TPU v7x, 32 devices: a whole 2x2x4 slice. The times are simulated.
32 devices in a mesh: seq: 8 (over y, x, core), fsdp: 4 (over z).
Axes of the slice: x: 2, y: 2, z: 4, core: 2. Of those that a mesh axis runs over, the one named last changes fastest.
Arguments:
- real_tokens: bfloat16 [4, 512, 3072], P('fsdp', 'seq'), may hold values from -6 to 6
- gen_hidden: bfloat16 [4, 512, 3072], P('fsdp', 'seq'), may hold values from -6 to 6
- modulation: float32 [4, 2, 3072], P('fsdp'), may hold values from -3 to 3
- norm_gain: float32 [3072], replicated, may hold values from 0.5 to 1.5
- proj_weight: bfloat16 [3, 3072, 2048], P(None, None, 'fsdp'), may hold values from -4 to 4
Outputs:
- grad_hidden: bfloat16 [4, 512, 3072], P('fsdp', 'seq')
All inputs are finite; a program needn't handle non-finite values.
Results may differ from a plain program's by a relative error of at most 0.012.
The roundings to bfloat16 on the way count: a program that leaves them out, or rounds other values in their place, can miss the bound.
Values may be sent and summed in bfloat16 or wider, within the bound.
A program may use at most 128 MiB of HBM per device.

v0:
```python
import jax
import jax.numpy as jnp
from jax import lax
from jax.sharding import PartitionSpec as P

HEADS = 16
HEAD_DIM = 128


norm_eps = 1e-06
match_eps = 0.05
loss_weight = 4.0


def to_wide(values):
    return lax.optimization_barrier(values).astype(jnp.float32)


def normalize(tokens, norm_gain):
    values = to_wide(tokens)
    inverse = lax.rsqrt(jnp.mean(values * values, axis=-1, keepdims=True) + norm_eps)
    return ((values * inverse * norm_gain).astype(jnp.bfloat16), inverse)


def attend(queries, key_rows, value_rows):
    scores = jnp.einsum(
        "qhd,khd->hqk", queries, key_rows, preferred_element_type=jnp.float32
    ) * HEAD_DIM ** (-0.5)
    highest = jnp.max(scores, axis=-1, keepdims=True)
    weights = jnp.exp(scores - highest)
    totals = jnp.sum(weights, axis=-1, keepdims=True)
    mixed_values = jnp.einsum(
        "hqk,khd->qhd", weights.astype(jnp.bfloat16), value_rows, preferred_element_type=jnp.float32
    )
    outputs = mixed_values / jnp.transpose(totals, (1, 0, 2))
    return (outputs, highest + jnp.log(totals))


def match_grad(fake_out, real_out):
    differ = fake_out - real_out
    return (loss_weight * differ / jnp.sqrt(differ * differ + match_eps * match_eps)).astype(
        jnp.bfloat16
    )


def row_delta(grad_out, fake_out):
    return jnp.sum(to_wide(grad_out) * fake_out, axis=-1)


def backward_scores(queries, key_rows, value_rows, log_total, deltas, grad_out):
    scores = jnp.einsum(
        "qhd,khd->hqk", queries, key_rows, preferred_element_type=jnp.float32
    ) * HEAD_DIM ** (-0.5)
    probs = jnp.exp(scores - log_total)
    dprobs = jnp.einsum("qhd,khd->hqk", grad_out, value_rows, preferred_element_type=jnp.float32)
    dscores = (probs * (dprobs - jnp.transpose(deltas)[:, :, None]) * HEAD_DIM ** (-0.5)).astype(
        jnp.bfloat16
    )
    return (probs.astype(jnp.bfloat16), dscores)


def on_device(real_tokens, gen_hidden, modulation, norm_gain, proj_weight):
    tok_count = real_tokens.shape[1]
    head_width = HEADS * HEAD_DIM
    fake_tokens = (
        gen_hidden[0].astype(jnp.float32) * (1.0 + modulation[0, 0]) + modulation[0, 1]
    ).astype(jnp.bfloat16)
    real_normed, real_inverse = normalize(real_tokens[0], norm_gain)
    fake_normed, fake_inverse = normalize(fake_tokens, norm_gain)
    both_normed = jnp.concatenate([real_normed, fake_normed], axis=0)
    projected = jnp.einsum(
        "td,kdc->ktc",
        lax.all_gather(both_normed, "fsdp", axis=0, tiled=True),
        proj_weight,
        preferred_element_type=jnp.float32,
    ).astype(jnp.bfloat16)
    mapped = lax.all_to_all(projected, "fsdp", split_axis=1, concat_axis=2, tiled=True)
    mapped = mapped.reshape(3, 2, tok_count, HEADS, HEAD_DIM)
    spread = lax.all_to_all(mapped, "seq", split_axis=3, concat_axis=2, tiled=True)
    real_out, real_total = attend(spread[0, 0], spread[1, 0], spread[2, 0])
    fake_out, fake_total = attend(spread[0, 1], spread[1, 1], spread[2, 1])
    grad_out = match_grad(fake_out, real_out)
    deltas = row_delta(grad_out, fake_out)
    prob_low, dscores = backward_scores(
        spread[0, 1], spread[1, 1], spread[2, 1], fake_total, deltas, grad_out
    )
    grad_query = jnp.einsum(
        "hqk,khd->qhd", dscores, spread[1, 1], preferred_element_type=jnp.float32
    )
    grad_key = jnp.einsum("hqk,qhd->khd", dscores, spread[0, 1], preferred_element_type=jnp.float32)
    grad_value = jnp.einsum("hqk,qhd->khd", prob_low, grad_out, preferred_element_type=jnp.float32)
    local_grads = jnp.stack([grad_query, grad_key, grad_value]).astype(jnp.bfloat16)
    all_grads = lax.all_to_all(local_grads, "seq", split_axis=1, concat_axis=2, tiled=True).reshape(
        3, tok_count, head_width
    )
    owner_grads = lax.all_to_all(all_grads, "fsdp", split_axis=2, concat_axis=1, tiled=True)
    grad_normed = lax.psum_scatter(
        jnp.einsum("ktc,kdc->td", owner_grads, proj_weight, preferred_element_type=jnp.float32),
        "fsdp",
        scatter_dimension=0,
        tiled=True,
    )
    scaled = to_wide(fake_tokens) * fake_inverse
    grad_scaled = grad_normed * norm_gain
    grad_fake = fake_inverse * (
        grad_scaled - scaled * jnp.mean(grad_scaled * scaled, axis=-1, keepdims=True)
    )
    grad_hidden = (grad_fake * (1.0 + modulation[0, 0])).astype(jnp.bfloat16)
    return grad_hidden[None]


def solution(mesh):
    placed = (
        P("fsdp", "seq", None),
        P("fsdp", "seq", None),
        P("fsdp", None, None),
        P(),
        P(None, None, "fsdp"),
    )
    return jax.shard_map(
        on_device, mesh=mesh, in_specs=placed, out_specs=P("fsdp", "seq", None), check_vma=False
    )
```

profile of v0, /device:TPU:20, one launch (start us, length us, event | category | flops | bytes accessed | tf_op | source)
XLA Modules:
  0.0 293.1 jit_solution(12995739763302523674)
XLA Ops:
  6.5 0.0 all-gather.2.cloned.1.call-start
  6.5 1.2 fusion.36
  7.7 0.8 slice_add_fusion
  8.6 1.1 fusion.40
  9.7 0.2 fusion.35
  9.9 1.3 fusion.38
  11.1 0.9 pad_maximum_fusion
  12.1 0.0 all-gather.2.cloned.1.call-update
  12.1 0.0 reduce-scatter.2.cloned.1.call-start
  12.1 63.3 %all-gather.2.cloned.1.call-done = bf16[512,3072]{1,0:T(8,128)(2,1)} async-done(((bf16[128,3072]{1,0:T(8,128)(2,1)}), bf16[512,3072]{1,0:T(8,128)(2,1)}) %all-gather.2.cloned.1.call-update) | async-done | bytes 3145744 | tf_op jit(solution)/shard_map/all_gather | solution.py:73
  75.4 9.4 %fusion.10 = bf16[3,512,512]{2,1,0:T(8,128)(2,1)S(1)} fusion(bf16[3,3072,512]{2,1,0:T(8,128)(2,1)} %param.9, bf16[512,3072]{1,0:T(8,128)(2,1)} %all-gather.2.cloned.1.call-done), kind=kOutput, calls=%fused_computation.16 | convolution fusion | flops 4832624640 | bytes 14155776 | tf_op jit(solution)/shard_map/td,kdc->ktc/dot_general | solution.py:71
  84.8 1.4 copy.34
  86.2 50.1 %all_to_all.66 = bf16[3,512,512]{2,0,1:T(4,128)(2,1)S(1)} all-to-all(bf16[3,512,512]{2,0,1:T(4,128)(2,1)S(1)} %copy.34), channel_id=1, replica_groups=mesh['seq'=8,'fsdp'=4] {'fsdp'}, dimensions={1} | all-to-all | bytes 3145728 | tf_op jit(solution)/shard_map/all_to_all | solution.py:77
  136.2 1.5 copy.73
  137.7 0.6 reshape.50
  138.4 0.4 copy.36
  138.8 23.5 %all_to_all.67 = bf16[3,2,64,16,128]{4,2,1,0,3:T(8,128)(2,1)S(1)} all-to-all(bf16[3,2,64,16,128]{4,2,1,0,3:T(8,128)(2,1)S(1)} %copy.36), channel_id=1, replica_groups=mesh['seq'=8,'fsdp'=4] {'seq'}, dimensions={3} | all-to-all | bytes 3145728 | tf_op jit(solution)/shard_map/all_to_all | solution.py:79
  162.3 0.2 copy.38
  162.5 0.4 multiply_reduce_fusion
  162.9 0.4 fusion.46
  163.4 0.3 fusion.3
  163.7 0.5 fusion.15
  164.2 0.4 fusion.5
  164.5 0.6 multiply_convert_fusion.1
  165.1 0.1 multiply_reduce_fusion.1
  165.2 0.5 fusion.18
  165.7 0.6 multiply_convert_fusion
  166.3 0.5 fusion.17
  166.8 0.3 fusion.16
  167.1 0.1 pad_maximum_fusion.1
  167.2 1.1 copy.50
  168.3 15.0 %all_to_all.68 = bf16[3,512,2,128]{3,2,0,1:T(2,128)(2,1)S(1)} all-to-all(bf16[3,512,2,128]{3,2,0,1:T(2,128)(2,1)S(1)} %copy.50), channel_id=1, replica_groups=mesh['seq'=8,'fsdp'=4] {'seq'}, dimensions={1} | all-to-all | bytes 1572864 | tf_op jit(solution)/shard_map/all_to_all | solution.py:93
  183.3 0.1 copy.51
  183.4 1.3 copy.68
  184.8 1.5 reshape.55
  186.3 22.8 %all_to_all.69 = bf16[4,2,49152]{2,1,0:T(2,128)(2,1)} all-to-all(bf16[4,2,49152]{2,1,0:T(2,128)(2,1)S(1)} %reshape.55), channel_id=1, replica_groups=mesh['seq'=8,'fsdp'=4] {'fsdp'}, dimensions={0} | all-to-all | bytes 1572864 | tf_op jit(solution)/shard_map/all_to_all | solution.py:96
  209.1 2.9 reshape.56
  212.0 1.1 copy.55
  213.1 8.0 %convolution_bitcast_fusion = f32[256,3072]{1,0:T(8,128)} fusion(bf16[3,256,512]{2,1,0:T(8,128)(2,1)S(1)} %bitcast.124, bf16[3,3072,512]{2,1,0:T(8,128)(2,1)} %param.9), kind=kOutput, calls=%fused_computation | convolution fusion | flops 2415919104 | bytes 13369344 | tf_op jit(solution)/shard_map/ktc,kdc->td/dot_general | solution.py:98
  221.1 0.0 copy-start
  221.1 0.0 reduce-scatter.2.cloned.1.call-update
  221.1 61.5 %reduce-scatter.2.cloned.1.call-done = f32[64,3072]{1,0:T(8,128)} async-done(((f32[256,3072]{1,0:T(8,128)}), f32[64,3072]{1,0:T(8,128)}) %reduce-scatter.2.cloned.1.call-update) | async-done | bytes 786448 | tf_op jit(solution)/shard_map/reduce_scatter | solution.py:97
  282.7 0.0 copy-done
  282.7 1.4 fusion.30
  284.1 2.1 fusion.43
  (3 shorter events, 0.0 us)
Async XLA Ops:
  6.5 68.9 %all-gather.2.cloned.1.call-start = ((), (), s32[]{:S(2)}) async-start(), calls=%async_computation.5 | async-start | bytes 3932160 | tf_op jit(solution)/shard_map/all_gather | solution.py:73
  12.1 270.6 %reduce-scatter.2.cloned.1.call-start = ((), (), s32[]{:S(2)}) async-start(), calls=%async_computation.6 | async-start | bytes 3932160 | tf_op jit(solution)/shard_map/reduce_scatter | solution.py:97
  221.1 61.6 %copy-start = (f32[3072]{0:T(1024)S(1)}, f32[3072]{0:T(1024)}, u32[]{:S(2)}) copy-start(f32[3072]{0:T(1024)} %param.8) | copy-start | bytes 36868
Sparse Core Ops, SparseCore 0:
  12.2 63.1 all-gather.1
  221.3 61.3 reduce-scatter.1
where the time goes:
time: 295 us; the launch traced here: 293 us
  waiting for transfers between devices  125 us (42%)
  blocking collectives  111 us (38%)
  matrix products  21.2 us (7%)
  between operations  13.6 us (5%)
  local copies, waits for them, and re-layouts  12.1 us (4%)
  other arithmetic  9.92 us (3%)
    all_gather x1, waiting for transfers between devices, on_device(): lax.all_gather(both_normed, 'fsdp', axis=0, tiled=True)  63.3 us
    reduce_scatter x1, waiting for transfers between devices, on_device(): lax.psum_scatter(jnp.einsum('ktc,kdc->td', owner_grads, proj_weight, pref...  61.5 us
    all_to_all x1, blocking collectives, on_device(): lax.all_to_all(projected, 'fsdp', split_axis=1, concat_axis=2, tiled=True)  50.1 us
    all_to_all x1, blocking collectives, on_device(): lax.all_to_all(mapped, 'seq', split_axis=3, concat_axis=2, tiled=True)  23.5 us
    all_to_all x1, blocking collectives, on_device(): lax.all_to_all(all_grads, 'fsdp', split_axis=2, concat_axis=1, tiled=True)  22.8 us
    all_to_all x1, blocking collectives, on_device(): lax.all_to_all(local_grads, 'seq', split_axis=1, concat_axis=2, tiled=True)  15 us
    dot_general x1, matrix products, on_device(): jnp.einsum('td,kdc->ktc', lax.all_gather(both_normed, 'fsdp', axis=0, til...  9.38 us
    dot_general x1, matrix products, on_device(): jnp.einsum('ktc,kdc->td', owner_grads, proj_weight, preferred_element_typ...  7.98 us
  transfers between devices with their start and end apart: 2, of which 2 were waited for; matrix products, arithmetic and copies ran while one was open for 0% of the time, Pallas kernels for 0%

commit v1 on v0

--- a/solution.py
+++ b/solution.py
@@ -3,7 +3,6 @@
 from jax import lax
 from jax.sharding import PartitionSpec as P
 
-HEADS = 16
 HEAD_DIM = 128
 
 
@@ -61,22 +60,26 @@
 
 def on_device(real_tokens, gen_hidden, modulation, norm_gain, proj_weight):
     tok_count = real_tokens.shape[1]
-    head_width = HEADS * HEAD_DIM
     fake_tokens = (
         gen_hidden[0].astype(jnp.float32) * (1.0 + modulation[0, 0]) + modulation[0, 1]
     ).astype(jnp.bfloat16)
     real_normed, real_inverse = normalize(real_tokens[0], norm_gain)
     fake_normed, fake_inverse = normalize(fake_tokens, norm_gain)
-    both_normed = jnp.concatenate([real_normed, fake_normed], axis=0)
+    both_normed = jnp.stack([real_normed, fake_normed])
+    group, ranks = lax.axis_size("fsdp"), lax.axis_size("seq")
+    owned = proj_weight.shape[2] // HEAD_DIM
+    each = group * owned // ranks
     projected = jnp.einsum(
-        "td,kdc->ktc",
-        lax.all_gather(both_normed, "fsdp", axis=0, tiled=True),
-        proj_weight,
+        "gstd,kdhc->ghkstc",
+        lax.all_gather(both_normed, "fsdp", axis=0),
+        proj_weight.reshape(proj_weight.shape[:2] + (owned, HEAD_DIM)),
         preferred_element_type=jnp.float32,
     ).astype(jnp.bfloat16)
-    mapped = lax.all_to_all(projected, "fsdp", split_axis=1, concat_axis=2, tiled=True)
-    mapped = mapped.reshape(3, 2, tok_count, HEADS, HEAD_DIM)
-    spread = lax.all_to_all(mapped, "seq", split_axis=3, concat_axis=2, tiled=True)
+    projected = projected.reshape(ranks, each, 3, 2, tok_count, HEAD_DIM)
+    spread = lax.all_to_all(projected, "seq", split_axis=0, concat_axis=0)
+    spread = jnp.transpose(spread, (2, 3, 0, 4, 1, 5)).reshape(
+        3, 2, ranks * tok_count, each, HEAD_DIM
+    )
     real_out, real_total = attend(spread[0, 0], spread[1, 0], spread[2, 0])
     fake_out, fake_total = attend(spread[0, 1], spread[1, 1], spread[2, 1])
     grad_out = match_grad(fake_out, real_out)
@@ -90,16 +93,19 @@
     grad_key = jnp.einsum("hqk,qhd->khd", dscores, spread[0, 1], preferred_element_type=jnp.float32)
     grad_value = jnp.einsum("hqk,qhd->khd", prob_low, grad_out, preferred_element_type=jnp.float32)
     local_grads = jnp.stack([grad_query, grad_key, grad_value]).astype(jnp.bfloat16)
-    all_grads = lax.all_to_all(local_grads, "seq", split_axis=1, concat_axis=2, tiled=True).reshape(
-        3, tok_count, head_width
-    )
-    owner_grads = lax.all_to_all(all_grads, "fsdp", split_axis=2, concat_axis=1, tiled=True)
+    local_grads = local_grads.reshape(3, ranks, tok_count, each, HEAD_DIM)
+    all_grads = lax.all_to_all(
+        jnp.transpose(local_grads, (1, 3, 0, 2, 4)), "seq", split_axis=0, concat_axis=0
+    ).reshape(group, owned, 3, tok_count, HEAD_DIM)
+    owner_grads = jnp.transpose(all_grads, (2, 0, 3, 1, 4)).reshape(3, group * tok_count, -1)
     grad_normed = lax.psum_scatter(
-        jnp.einsum("ktc,kdc->td", owner_grads, proj_weight, preferred_element_type=jnp.float32),
+        jnp.einsum(
+            "ktc,kdc->td", owner_grads, proj_weight, preferred_element_type=jnp.float32
+        ).astype(jnp.bfloat16),
         "fsdp",
         scatter_dimension=0,
         tiled=True,
-    )
+    ).astype(jnp.float32)
     scaled = to_wide(fake_tokens) * fake_inverse
     grad_scaled = grad_normed * norm_gain
     grad_fake = fake_inverse * (

time: 295 us -> 188 us (0.64)
  blocking collectives: 111 us -> 38.5 us
  waiting for transfers between devices: 125 us -> 82.7 us
  local copies, waits for them, and re-layouts: 12.1 us -> 16 us
    all_to_all x4 -> x2, blocking collectives: 111 us -> 38.5 us  [the longest x1 23.5 us: on_device(): spread = lax.all_to_all(projected, 'seq', split_axis=0, concat_axis=0)]
    reduce_scatter x1, waiting for transfers between devices: 61.5 us -> 33.5 us  [on_device(): lax.psum_scatter(jnp.einsum('ktc,kdc->td', owner_grads, proj_weight, pref...]
    all_gather x1, waiting for transfers between devices: 63.3 us -> 49.1 us  [on_device(): lax.all_gather(both_normed, 'fsdp', axis=0)]
    reshape x3 -> x2, local copies, waits for them, and re-layouts: 2.39 us -> 14.5 us  [the longest x1 14.2 us: on_device(): proj_weight.reshape(proj_weight.shape[:2] + (owned, HEAD_DIM))]
    unnamed x4 -> x2, local copies, waits for them, and re-layouts: 4.4 us -> 0.01 us
  transfers between devices with their start and end apart: 2 -> 2, of which waited for: 2 -> 2; matrix products, arithmetic and copies ran while one was open for 0% -> 8% of each run, Pallas kernels for 0% -> 0%
where the time goes in v1:
time: 188 us; the launch traced here: 185 us
  waiting for transfers between devices  82.7 us (44%)
  blocking collectives  38.5 us (20%)
  matrix products  24.1 us (13%)
  local copies, waits for them, and re-layouts  16 us (9%)
  between operations  13.6 us (7%)
  other arithmetic  9.7 us (5%)
    all_gather x1, waiting for transfers between devices, on_device(): lax.all_gather(both_normed, 'fsdp', axis=0)  49.1 us
    reduce_scatter x1, waiting for transfers between devices, on_device(): lax.psum_scatter(jnp.einsum('ktc,kdc->td', owner_grads, proj_weight, pref...  33.5 us
    all_to_all x1, blocking collectives, on_device(): spread = lax.all_to_all(projected, 'seq', split_axis=0, concat_axis=0)  23.5 us
    all_to_all x1, blocking collectives, on_device(): lax.all_to_all(jnp.transpose(local_grads, (1, 3, 0, 2, 4)), 'seq', split_...  15 us
    reshape x1, local copies, waits for them, and re-layouts, on_device(): proj_weight.reshape(proj_weight.shape[:2] + (owned, HEAD_DIM))  14.2 us
    dot_general x1, matrix products, on_device(): jnp.einsum('ktc,kdc->td', owner_grads, proj_weight, preferred_element_typ...  10.9 us
    dot_general x1, matrix products, on_device(): jnp.einsum('gstd,kdhc->ghkstc', lax.all_gather(both_normed, 'fsdp', axis=...  9.41 us
  transfers between devices with their start and end apart: 2, of which 2 were waited for; matrix products, arithmetic and copies ran while one was open for 8% of the time, Pallas kernels for 0%

profile of v1, /device:TPU:20, one launch (start us, length us, event | category | flops | bytes accessed | tf_op | source)
XLA Modules:
  0.0 184.6 jit_solution(16817842815229260254)
XLA Ops:
  6.5 0.0 all-gather.3.cloned.1.call-start
  6.5 1.2 fusion.37
  7.7 0.8 slice_add_fusion
  8.6 1.1 fusion.41
  9.7 0.2 fusion.36
  9.9 1.3 fusion.44
  11.1 1.0 pad_maximum_fusion
  12.1 0.0 all-gather.3.cloned.1.call-update
  12.2 0.0 reduce-scatter.2.cloned.1.call-start
  12.2 14.2 %reshape.67 = bf16[3,3072,4,128]{3,2,1,0:T(4,128)(2,1)} reshape(bf16[3,3072,512]{2,1,0:T(8,128)(2,1)} %param.9) | data formatting | bytes 18874368 | tf_op jit(solution)/shard_map/reshape | solution.py:75
  26.4 49.1 %all-gather.3.cloned.1.call-done = bf16[8,64,3072]{2,1,0:T(8,128)(2,1)} async-done(((bf16[2,64,3072]{2,1,0:T(8,128)(2,1)}), bf16[8,64,3072]{2,1,0:T(8,128)(2,1)}) %all-gather.3.cloned.1.call-update) | async-done | bytes 3145744 | tf_op jit(solution)/shard_map/all_gather | solution.py:74
  75.5 9.4 %fusion.11 = bf16[4,4,3,2,64,128]{5,4,1,2,3,0:T(8,128)(2,1)S(1)} fusion(bf16[4,2,64,3072,1,1]{3,2,5,4,1,0:T(8,128)(2,1)} %bitcast.122, bf16[3,3072,4,128,1,1]{3,2,1,0,5,4:T(4,128)(2,1)} %bitcast.100), kind=kOutput, calls=%fused_computation.16 | convolution fusion | flops 4832624640 | bytes 14155776 | tf_op jit(solution)/shard_map/gstd,kdhc->ghkstc/dot_general | solution.py:72
  84.9 0.1 copy.38
  85.0 23.5 %all_to_all.10 = bf16[8,2,3,2,64,128]{5,4,3,2,1,0:T(8,128)(2,1)S(1)} all-to-all(bf16[8,2,3,2,64,128]{5,4,3,2,1,0:T(8,128)(2,1)S(1)} %bitcast.108), channel_id=1, replica_groups=mesh['seq'=8,'fsdp'=4] {'seq'}, dimensions={0} | all-to-all | bytes 3145728 | tf_op jit(solution)/shard_map/all_to_all | solution.py:79
  108.6 0.2 copy.39
  108.7 0.4 multiply_reduce_fusion
  109.2 0.4 fusion.49
  109.6 0.3 fusion.4
  110.0 0.5 fusion.16
  110.4 0.4 fusion.6
  110.8 0.6 multiply_convert_fusion.1
  111.4 0.1 multiply_reduce_fusion.1
  111.4 0.5 fusion.19
  111.9 0.6 multiply_convert_fusion
  112.5 0.5 fusion.18
  113.0 0.3 fusion.17
  113.4 0.2 copy.53
  113.5 0.2 copy.48
  113.7 0.2 copy.51
  113.9 0.1 maximum_bitcast_fusion
  114.0 0.1 copy.54
  114.0 15.0 %all_to_all.11 = bf16[8,2,3,64,128]{4,3,1,2,0:T(8,128)(2,1)S(1)} all-to-all(bf16[8,2,3,64,128]{4,3,1,2,0:T(8,128)(2,1)S(1)} %copy.54), channel_id=1, replica_groups=mesh['seq'=8,'fsdp'=4] {'seq'}, dimensions={0} | all-to-all | bytes 1572864 | tf_op jit(solution)/shard_map/all_to_all | solution.py:97
  129.0 0.1 copy.55
  129.1 0.6 copy.56
  129.7 0.3 reshape.71
  130.0 0.0 copy-start
  130.0 10.9 %fusion.2 = bf16[256,3072]{1,0:T(8,128)(2,1)} fusion(bf16[3,256,512]{2,1,0:T(8,128)(2,1)S(1)} %reshape.71, bf16[3,3072,512]{2,1,0:T(8,128)(2,1)} %param.9), kind=kOutput, calls=%fused_computation.3 | convolution fusion | flops 2416705536 | bytes 11796480 | tf_op jit(solution)/shard_map/ktc,kdc->td/dot_general | solution.py:102
  140.9 0.0 reduce-scatter.2.cloned.1.call-update
  141.0 33.5 %reduce-scatter.2.cloned.1.call-done = bf16[64,3072]{1,0:T(8,128)(2,1)} async-done(((bf16[256,3072]{1,0:T(8,128)(2,1)}), bf16[64,3072]{1,0:T(8,128)(2,1)}) %reduce-scatter.2.cloned.1.call-update) | async-done | bytes 393232 | tf_op jit(solution)/shard_map/reduce_scatter | solution.py:101
  174.5 0.0 copy-done
  174.5 1.3 fusion.31
  175.8 2.0 %fusion.45 = bf16[1,64,3072]{2,1,0:T(8,128)(2,1)} fusion(bf16[64,3072]{1,0:T(8,128)(2,1)S(1)} %fusion.41, bf16[64,3072]{1,0:T(8,128)(2,1)} %reduce-scatter.2.cloned.1.call-done, f32[64]{0:T(128)S(1)} %broadcast_multiply_fusion, f32[3072]{0:T(1024)S(1)} %copy-done, f32[64]{0:T(128)S(1)} %get-tuple-element.14, f32[3072]{0:T(1024)S(1)} %bitcast.117), kind=kLoop, calls=%fused_computation.58 | loop fusion | flops 1769472 | bytes 1204736 | tf_op jit(solution)/shard_map/broadcast_in_dim | solution.py:115
  (3 shorter events, 0.0 us)
Async XLA Ops:
  6.5 69.0 %all-gather.3.cloned.1.call-start = ((), (), s32[]{:S(2)}) async-start(), calls=%async_computation.4 | async-start | bytes 3932160 | tf_op jit(solution)/shard_map/all_gather | solution.py:74
  12.2 162.3 %reduce-scatter.2.cloned.1.call-start = ((), (), s32[]{:S(2)}) async-start(), calls=%async_computation.3 | async-start | bytes 1966080 | tf_op jit(solution)/shard_map/reduce_scatter | solution.py:101
  130.0 44.5 %copy-start = (f32[3072]{0:T(1024)S(1)}, f32[3072]{0:T(1024)}, u32[]{:S(2)}) copy-start(f32[3072]{0:T(1024)} %param.8) | copy-start | bytes 36868
Sparse Core Ops, SparseCore 0:
  12.3 63.1 all-gather.2
  141.1 33.3 reduce-scatter.1

commit v2 on v0

v2 whole, which is shorter than its diff:
```python
import functools

import jax
import jax.numpy as jnp
from jax import lax
from jax.experimental import pallas as pl
from jax.experimental.pallas import tpu as pltpu
from jax.sharding import PartitionSpec as P

HEAD_DIM = 128
norm_eps = 1e-06
match_eps = 0.05
loss_weight = 4.0
MESH = pl.DeviceIdType.MESH
NT = (((1,), (1,)), ((), ()))
TN = (((0,), (0,)), ((), ()))


def mm(a, b, dims=(((1,), (0,)), ((), ()))):
    return lax.dot_general(a, b, dims, preferred_element_type=jnp.float32)


def kernel(
    group, ranks, owned, each,
    real_ref, hidden_ref, mod_ref, gain_ref, weight_ref, out_ref,
    weight, gath, tokens, inverse, stage, qkv, grad_key, grad_value, gstage, grecv,
    partial, sums, arrived,
    weight_sem, ag_send, ag_recv, fw_send, fw_recv, bw_send, bw_recv, rs_send, rs_recv,
):
    me, plane = lax.axis_index("seq"), lax.axis_index("fsdp")
    count, width = real_ref.shape[1], real_ref.shape[2]
    length = ranks * count
    pairs = group * owned
    scale = HEAD_DIM ** (-0.5)
    columns = owned * HEAD_DIM

    barrier = pltpu.get_barrier_semaphore()
    for other in range(ranks):
        @pl.when(other != me)
        def _():
            pl.semaphore_signal(barrier, inc=1, device_id={"seq": other}, device_id_type=MESH)

    @pl.when(plane > 0)
    def _():
        pl.semaphore_signal(barrier, inc=1, device_id={"fsdp": plane - 1}, device_id_type=MESH)

    @pl.when(plane < group - 1)
    def _():
        pl.semaphore_signal(barrier, inc=1, device_id={"fsdp": plane + 1}, device_id_type=MESH)

    loads = [pltpu.make_async_copy(weight_ref.at[k], weight.at[k], weight_sem.at[k]) for k in range(3)]
    for load in loads:
        load.start()

    rows_each = 16
    scale_row = 1.0 + mod_ref[0, 0:1, :]
    shift_row = mod_ref[0, 1:2, :]

    def normed_rows(values):
        inv = lax.rsqrt(jnp.mean(values * values, axis=-1, keepdims=True) + norm_eps)
        return (values * inv * gain_ref[...]).astype(jnp.bfloat16), inv

    @pl.loop(0, count // rows_each)
    def _(i):
        rows = pl.ds(pl.multiple_of(i * rows_each, rows_each), rows_each)
        gath[plane, 0, rows, :] = normed_rows(real_ref[0, rows, :].astype(jnp.float32))[0]

    peers = ranks - 1 + (plane > 0).astype(jnp.int32) + (plane < group - 1).astype(jnp.int32)
    pl.semaphore_wait(barrier, peers)

    toward = (plane + 1, plane - 1)
    has_next = (plane < group - 1, plane > 0)
    has_prev = (plane > 0, plane < group - 1)

    def handed(way, hop, stream, block):
        return pltpu.make_async_remote_copy(
            src_ref=gath.at[block, stream], dst_ref=gath.at[block, stream],
            send_sem=ag_send.at[way, hop, stream], recv_sem=ag_recv.at[way, hop, stream],
            device_id={"fsdp": toward[way]}, device_id_type=MESH,
        )

    def sent_block(way, hop):
        return plane - hop if way == 0 else plane + hop

    def got_block(way, hop):
        return plane - 1 - hop if way == 0 else plane + 1 + hop

    def inside(block):
        return (block >= 0) & (block < group)

    def give(way, hop, stream):
        @pl.when(has_next[way] & inside(sent_block(way, hop)))
        def _():
            handed(way, hop, stream, sent_block(way, hop)).start()

    def forward_copy(stream, pair):
        return pltpu.make_async_remote_copy(
            src_ref=stage.at[stream, pair], dst_ref=qkv.at[lax.rem(pair, each), stream, :, me],
            send_sem=fw_send.at[stream, pair], recv_sem=fw_recv.at[stream, lax.rem(pair, each), me],
            device_id={"seq": lax.div(pair, each)}, device_id_type=MESH,
        )

    wide = min(256, columns)

    def project(block, stream):
        @pl.loop(0, 3 * (columns // wide))
        def _(i):
            k, tile = lax.div(i, columns // wide), lax.rem(i, columns // wide)
            cols = pl.ds(pl.multiple_of(tile * wide, wide), wide)
            done = mm(gath[block, stream], weight[k, :, cols]).astype(jnp.bfloat16)
            for h in range(wide // HEAD_DIM):
                pair = block * owned + tile * (wide // HEAD_DIM) + h
                stage[stream, pair, k] = done[:, h * HEAD_DIM : (h + 1) * HEAD_DIM]

        for j in range(owned):
            pair = block * owned + j

            @pl.when(lax.div(pair, each) != me)
            def _():
                forward_copy(stream, pair).start()

            @pl.when(lax.div(pair, each) == me)
            def _():
                e = lax.rem(pair, each)
                pltpu.make_async_copy(
                    stage.at[stream, pair], qkv.at[e, stream, :, me], fw_recv.at[stream, e, me]
                ).start()

    for way in range(2):
        give(way, 0, 0)

    @pl.loop(0, count // rows_each)
    def _(i):
        rows = pl.ds(pl.multiple_of(i * rows_each, rows_each), rows_each)
        fake = (hidden_ref[0, rows, :].astype(jnp.float32) * scale_row + shift_row).astype(jnp.bfloat16)
        tokens[rows, :] = fake
        normed, inv = normed_rows(fake.astype(jnp.float32))
        gath[plane, 1, rows, :] = normed
        inverse[rows, :] = jnp.broadcast_to(inv, (rows_each, HEAD_DIM))

    for way in range(2):
        give(way, 0, 1)
    for load in loads:
        load.wait()

    @pl.loop(0, 2)
    def _(stream):
        project(plane, stream)

    @pl.loop(0, 2 * (group - 1))
    def _(step):
        hop, stream = lax.div(step, 2), lax.rem(step, 2)
        for way in range(2):
            @pl.when(inside(got_block(way, hop)))
            def _():
                handed(way, hop, stream, got_block(way, hop)).wait_recv()

                @pl.when(hop + 1 < group - 1)
                def _():
                    give(way, hop + 1, stream)

        for way in range(2):
            @pl.when(inside(got_block(way, hop)))
            def _():
                project(got_block(way, hop), stream)

    block_rows = 256 if length % 256 == 0 else length
    block_parts = block_rows // count

    def flat(values):
        return values.reshape(-1, HEAD_DIM)

    def back_copy(e, other):
        return pltpu.make_async_remote_copy(
            src_ref=gstage.at[e, :, other], dst_ref=grecv.at[me * each + e],
            send_sem=bw_send.at[e, other], recv_sem=bw_recv.at[me * each + e],
            device_id={"seq": other}, device_id_type=MESH,
        )

    @pl.loop(0, each)
    def _(e):
        for stream in range(2):
            @pl.loop(0, ranks)
            def _(source):
                pltpu.make_async_copy(
                    stage.at[stream, 0], qkv.at[e, stream, :, source], fw_recv.at[stream, e, source]
                ).wait()

        grad_key[...] = jnp.zeros_like(grad_key)
        grad_value[...] = jnp.zeros_like(grad_value)

        @pl.loop(0, length // block_rows)
        def _(b):
            parts = pl.ds(b * block_parts, block_parts)

            def attend(stream):
                queries = flat(qkv[e, stream, 0, parts])
                scores = mm(queries, flat(qkv[e, stream, 1]), NT) * scale
                weights = jnp.exp(scores - jnp.max(scores, axis=-1, keepdims=True))
                share = 1.0 / jnp.sum(weights, axis=-1, keepdims=True)
                mixed = mm(weights.astype(jnp.bfloat16), flat(qkv[e, stream, 2])) * share
                return queries, weights, share, mixed

            real_out = attend(0)[3]
            queries, weights, share, fake_out = attend(1)
            differ = fake_out - real_out
            grad_out = (loss_weight * differ * lax.rsqrt(differ * differ + match_eps * match_eps)).astype(jnp.bfloat16)
            deltas = jnp.sum(grad_out.astype(jnp.float32) * fake_out, axis=-1, keepdims=True)
            probs = weights * share
            dprobs = mm(grad_out, flat(qkv[e, 1, 2]), NT)
            dscores = (probs * (dprobs - deltas) * scale).astype(jnp.bfloat16)
            grad_query = mm(dscores, flat(qkv[e, 1, 1])).astype(jnp.bfloat16)
            gstage[e, 0, parts] = grad_query.reshape(block_parts, count, HEAD_DIM)
            grad_key[...] += mm(dscores, queries, TN)
            grad_value[...] += mm(probs.astype(jnp.bfloat16), grad_out, TN)

        gstage[e, 1] = grad_key[...].astype(jnp.bfloat16).reshape(ranks, count, HEAD_DIM)
        gstage[e, 2] = grad_value[...].astype(jnp.bfloat16).reshape(ranks, count, HEAD_DIM)

        @pl.loop(0, ranks)
        def _(other):
            @pl.when(other != me)
            def _():
                back_copy(e, other).start()

            @pl.when(other == me)
            def _():
                pltpu.make_async_copy(
                    gstage.at[e, :, me], grecv.at[me * each + e], bw_recv.at[me * each + e]
                ).start()

    deep = 512 if width % 512 == 0 else width

    def grad_rows(block):
        for j in range(owned):
            pair = block * owned + j
            pltpu.make_async_copy(gstage.at[0, :, 0], grecv.at[pair], bw_recv.at[pair]).wait()

        @pl.loop(0, width // deep)
        def _(i):
            at = pl.ds(pl.multiple_of(i * deep, deep), deep)
            total = None
            for k in range(3):
                rows = jnp.concatenate([grecv[block * owned + j, k] for j in range(owned)], axis=1)
                term = mm(rows, weight[k, at, :], NT)
                total = term if total is None else total + term
            partial[:, at] = total

    def sum_copy(way, block):
        return pltpu.make_async_remote_copy(
            src_ref=sums.at[block], dst_ref=arrived.at[way, block],
            send_sem=rs_send.at[way, block], recv_sem=rs_recv.at[way, block],
            device_id={"fsdp": toward[way]}, device_id_type=MESH,
        )

    def add_arrived(way, block):
        @pl.when(has_prev[way])
        def _():
            sum_copy(way, block).wait_recv()
            partial[...] += arrived[way, block].astype(jnp.float32)

    @pl.loop(0, group - 1)
    def _(step):
        for way in range(2):
            block = group - 1 - step if way == 0 else step

            @pl.when((block > plane) if way == 0 else (block < plane))
            def _():
                grad_rows(block)
                add_arrived(way, block)
                sums[block] = partial[...].astype(jnp.bfloat16)
                sum_copy(way, block).start()

    grad_rows(plane)
    for way in range(2):
        add_arrived(way, plane)

    @pl.loop(0, count // rows_each)
    def _(i):
        rows = pl.ds(pl.multiple_of(i * rows_each, rows_each), rows_each)
        inv = inverse[rows, 0:1]
        scaled = tokens[rows, :].astype(jnp.float32) * inv
        grad_scaled = partial[rows, :] * gain_ref[...]
        mean = jnp.mean(grad_scaled * scaled, axis=-1, keepdims=True)
        out_ref[0, rows, :] = (inv * (grad_scaled - scaled * mean) * scale_row).astype(jnp.bfloat16)

    for way in range(2):
        @pl.loop(0, group - 1)
        def _(hop):
            @pl.when(has_next[way] & inside(sent_block(way, hop)))
            def _():
                for stream in range(2):
                    handed(way, hop, stream, sent_block(way, hop)).wait_send()

        @pl.loop(0, group)
        def _(block):
            @pl.when((block > plane) if way == 0 else (block < plane))
            def _():
                sum_copy(way, block).wait_send()

    @pl.loop(0, pairs)
    def _(pair):
        @pl.when(lax.div(pair, each) != me)
        def _():
            for stream in range(2):
                forward_copy(stream, pair).wait_send()

    @pl.loop(0, ranks)
    def _(other):
        @pl.when(other != me)
        def _():
            for e in range(each):
                back_copy(e, other).wait_send()


def on_device(group, ranks, real_tokens, gen_hidden, modulation, norm_gain, proj_weight):
    _, count, width = real_tokens.shape
    columns = proj_weight.shape[2]
    owned = columns // HEAD_DIM
    pairs = group * owned
    each = pairs // ranks
    low, full = jnp.bfloat16, jnp.float32
    dma = pltpu.SemaphoreType.DMA
    vmem = pl.BlockSpec(memory_space=pltpu.VMEM)
    return pl.pallas_call(
        functools.partial(kernel, group, ranks, owned, each),
        out_shape=jax.ShapeDtypeStruct(real_tokens.shape, low),
        in_specs=[vmem] * 4 + [pl.BlockSpec(memory_space=pl.ANY)],
        out_specs=vmem,
        scratch_shapes=[
            pltpu.VMEM((3, width, columns), low),
            pltpu.VMEM((group, 2, count, width), low),
            pltpu.VMEM((count, width), low),
            pltpu.VMEM((count, HEAD_DIM), full),
            pltpu.VMEM((2, pairs, 3, count, HEAD_DIM), low),
            pltpu.VMEM((each, 2, 3, ranks, count, HEAD_DIM), low),
            pltpu.VMEM((ranks * count, HEAD_DIM), full),
            pltpu.VMEM((ranks * count, HEAD_DIM), full),
            pltpu.VMEM((each, 3, ranks, count, HEAD_DIM), low),
            pltpu.VMEM((pairs, 3, count, HEAD_DIM), low),
            pltpu.VMEM((count, width), full),
            pltpu.VMEM((group, count, width), low),
            pltpu.VMEM((2, group, count, width), low),
            dma((3,)),
            dma((2, group - 1, 2)),
            dma((2, group - 1, 2)),
            dma((2, pairs)),
            dma((2, each, ranks)),
            dma((each, ranks)),
            dma((pairs,)),
            dma((2, group)),
            dma((2, group)),
        ],
        compiler_params=pltpu.CompilerParams(
            collective_id=0, has_side_effects=True, vmem_limit_bytes=56 * 1024 * 1024
        ),
    )(real_tokens, gen_hidden, modulation, norm_gain.reshape(1, width), proj_weight)


def solution(mesh):
    placed = (
        P("fsdp", "seq", None),
        P("fsdp", "seq", None),
        P("fsdp", None, None),
        P(),
        P(None, None, "fsdp"),
    )
    return jax.shard_map(
        functools.partial(on_device, mesh.shape["fsdp"], mesh.shape["seq"]),
        mesh=mesh, in_specs=placed, out_specs=P("fsdp", "seq", None), check_vma=False,
    )
```

time: 295 us -> 134 us (0.45)
  Pallas kernels: 0 us -> 132 us
  waiting for transfers between devices: 125 us -> 0 us
  blocking collectives: 111 us -> 0 us
  matrix products: 21.2 us -> 0 us
  between operations: 13.6 us -> 0.01 us
  local copies, waits for them, and re-layouts: 12.1 us -> 1.77 us
  other arithmetic: 9.92 us -> 0 us
    pallas_call x0 -> x1, Pallas kernels: none -> 132 us  [on_device(): pl.pallas_call(functools.partial(kernel, group, ranks, owned, each), out_...]
    all_to_all x4 -> x0, blocking collectives: 111 us -> none  [the longest x1 50.1 us: on_device(): lax.all_to_all(projected, 'fsdp', split_axis=1, concat_axis=2, tiled=True)]
    all_gather x1 -> x0, waiting for transfers between devices: 63.3 us -> none  [on_device(): lax.all_gather(both_normed, 'fsdp', axis=0, tiled=True)]
    reduce_scatter x1 -> x0, waiting for transfers between devices: 61.5 us -> none  [on_device(): lax.psum_scatter(jnp.einsum('ktc,kdc->td', owner_grads, proj_weight, pref...]
    dot_general x10 -> x0, matrix products: 21.2 us -> none  [the longest x1 9.38 us: on_device(): jnp.einsum('td,kdc->ktc', lax.all_gather(both_normed, 'fsdp', axis=0, til...]
    reduce_sum x6 -> x0, other arithmetic: 3.53 us -> none  [the longest x1 1.42 us: on_device(): jnp.mean(grad_scaled * scaled, axis=-1, keepdims=True)]
  transfers between devices with their start and end apart: 2 -> 0, of which waited for: 2 -> 0; matrix products, arithmetic and copies ran while one was open for 0% -> 0% of each run, Pallas kernels for 0% -> 0%
where the time goes in v2:
time: 134 us
  Pallas kernels  132 us (99%)
  local copies, waits for them, and re-layouts  1.77 us (1%)
    pallas_call x1, Pallas kernels, on_device(): pl.pallas_call(functools.partial(kernel, group, ranks, owned, each), out_...  132 us

profile of v2, /device:TPU:20, one launch (start us, length us, event | category | flops | bytes accessed | tf_op | source)
XLA Modules:
  0.0 133.5 jit_solution(5123755347158211315)
XLA Ops:
  0.0 131.8 %shard_map.55 = bf16[1,64,3072]{2,1,0:T(8,128)(2,1)} custom-call(bf16[1,64,3072]{2,1,0:T(8,128)(2,1)} %real_ref.1, bf16[1,64,3072]{2,1,0:T(8,128)(2,1)} %hidden_ref.1, f32[1,2,3072]{2,1,0:T(2,128)} %mod_ref.1, f32[1,3072]{1,0:T(1,128)} %bitcast.1, bf16[3,3072,512]{2,1,0:T(8,128)(2,1)} %weight_ref.1), custom_call_target="tpu_custom_call" | custom-call | tf_op jit(solution)/shard_map/pallas_call | solution.py:325
  131.8 1.8 %copy.7 = bf16[1,64,3072]{2,1,0:T(8,128)(2,1)} copy(bf16[1,64,3072]{2,1,0:T(8,128)(2,1)} %shard_map.55) | data formatting | bytes 786432

commit v3 on v2

--- a/solution.py
+++ b/solution.py
@@ -70,7 +70,6 @@
 
     toward = (plane + 1, plane - 1)
     has_next = (plane < group - 1, plane > 0)
-    has_prev = (plane > 0, plane < group - 1)
 
     def handed(way, hop, stream, block):
         return pltpu.make_async_remote_copy(
@@ -109,11 +108,11 @@
             cols = pl.ds(pl.multiple_of(tile * wide, wide), wide)
             done = mm(gath[block, stream], weight[k, :, cols]).astype(jnp.bfloat16)
             for h in range(wide // HEAD_DIM):
-                pair = block * owned + tile * (wide // HEAD_DIM) + h
+                pair = (tile * (wide // HEAD_DIM) + h) * group + block
                 stage[stream, pair, k] = done[:, h * HEAD_DIM : (h + 1) * HEAD_DIM]
 
         for j in range(owned):
-            pair = block * owned + j
+            pair = j * group + block
 
             @pl.when(lax.div(pair, each) != me)
             def _():
@@ -217,23 +216,19 @@
         gstage[e, 1] = grad_key[...].astype(jnp.bfloat16).reshape(ranks, count, HEAD_DIM)
         gstage[e, 2] = grad_value[...].astype(jnp.bfloat16).reshape(ranks, count, HEAD_DIM)
 
-        @pl.loop(0, ranks)
-        def _(other):
-            @pl.when(other != me)
-            def _():
-                back_copy(e, other).start()
-
-            @pl.when(other == me)
-            def _():
-                pltpu.make_async_copy(
-                    gstage.at[e, :, me], grecv.at[me * each + e], bw_recv.at[me * each + e]
-                ).start()
+        @pl.loop(1, ranks)
+        def _(away):
+            back_copy(e, lax.rem(me + away, ranks)).start()
+
+        pltpu.make_async_copy(
+            gstage.at[e, :, me], grecv.at[me * each + e], bw_recv.at[me * each + e]
+        ).start()
 
     deep = 512 if width % 512 == 0 else width
 
     def grad_rows(block):
         for j in range(owned):
-            pair = block * owned + j
+            pair = j * group + block
             pltpu.make_async_copy(gstage.at[0, :, 0], grecv.at[pair], bw_recv.at[pair]).wait()
 
         @pl.loop(0, width // deep)
@@ -241,7 +236,7 @@
             at = pl.ds(pl.multiple_of(i * deep, deep), deep)
             total = None
             for k in range(3):
-                rows = jnp.concatenate([grecv[block * owned + j, k] for j in range(owned)], axis=1)
+                rows = jnp.concatenate([grecv[j * group + block, k] for j in range(owned)], axis=1)
                 term = mm(rows, weight[k, at, :], NT)
                 total = term if total is None else total + term
             partial[:, at] = total
@@ -250,30 +245,34 @@
         return pltpu.make_async_remote_copy(
             src_ref=sums.at[block], dst_ref=arrived.at[way, block],
             send_sem=rs_send.at[way, block], recv_sem=rs_recv.at[way, block],
-            device_id={"fsdp": toward[way]}, device_id_type=MESH,
+            device_id={"fsdp": jnp.where(way == 0, plane + 1, plane - 1)}, device_id_type=MESH,
         )
 
     def add_arrived(way, block):
-        @pl.when(has_prev[way])
+        @pl.when(((way == 0) & (plane > 0)) | ((way == 1) & (plane < group - 1)))
         def _():
             sum_copy(way, block).wait_recv()
             partial[...] += arrived[way, block].astype(jnp.float32)
 
-    @pl.loop(0, group - 1)
-    def _(step):
-        for way in range(2):
-            block = group - 1 - step if way == 0 else step
-
-            @pl.when((block > plane) if way == 0 else (block < plane))
-            def _():
-                grad_rows(block)
-                add_arrived(way, block)
-                sums[block] = partial[...].astype(jnp.bfloat16)
-                sum_copy(way, block).start()
+    near = (2 * plane > group - 1).astype(jnp.int32)
+
+    @pl.loop(0, 2 * (group - 1))
+    def _(turn):
+        step, way = lax.div(turn, 2), lax.rem(near + turn, 2)
+        block = jnp.where(way == 0, group - 1 - step, step)
+
+        @pl.when(((way == 0) & (block > plane)) | ((way == 1) & (block < plane)))
+        def _():
+            grad_rows(block)
+            add_arrived(way, block)
+            sums[block] = partial[...].astype(jnp.bfloat16)
+            sum_copy(way, block).start()
 
     grad_rows(plane)
-    for way in range(2):
-        add_arrived(way, plane)
+
+    @pl.loop(0, 2)
+    def _(turn):
+        add_arrived(lax.rem(near + turn, 2), plane)
 
     @pl.loop(0, count // rows_each)
     def _(i):

time: 134 us -> 114 us (0.85)
  Pallas kernels: 132 us -> 111 us
    pallas_call x1, Pallas kernels: 132 us -> 111 us  [on_device(): pl.pallas_call(functools.partial(kernel, group, ranks, owned, each), out_...]
where the time goes in v3:
time: 114 us; the launch traced here: 113 us
  Pallas kernels  111 us (97%)
  local copies, waits for them, and re-layouts  1.77 us (2%)
    pallas_call x1, Pallas kernels, on_device(): pl.pallas_call(functools.partial(kernel, group, ranks, owned, each), out_...  111 us

profile of v3, /device:TPU:20, one launch (start us, length us, event | category | flops | bytes accessed | tf_op | source)
XLA Modules:
  0.0 112.5 jit_solution(2329227133647696265)
XLA Ops:
  0.0 110.7 %shard_map.55 = bf16[1,64,3072]{2,1,0:T(8,128)(2,1)} custom-call(bf16[1,64,3072]{2,1,0:T(8,128)(2,1)} %real_ref.1, bf16[1,64,3072]{2,1,0:T(8,128)(2,1)} %hidden_ref.1, f32[1,2,3072]{2,1,0:T(2,128)} %mod_ref.1, f32[1,3072]{1,0:T(1,128)} %bitcast.1, bf16[3,3072,512]{2,1,0:T(8,128)(2,1)} %weight_ref.1), custom_call_target="tpu_custom_call" | custom-call | tf_op jit(solution)/shard_map/pallas_call | solution.py:324
  110.7 1.8 %copy.7 = bf16[1,64,3072]{2,1,0:T(8,128)(2,1)} copy(bf16[1,64,3072]{2,1,0:T(8,128)(2,1)} %shard_map.55) | data formatting | bytes 786432
